TPU v7x, 512 devices: a whole 4x4x16 slice. The times are simulated.
512 devices in a mesh: seq: 256 (over x, z, y_hi, core), sub: 2 (over y_lo).
Axes of the slice: x: 4, y: 4 (y_hi: 2, y_lo: 2; y = y_hi * 2 + y_lo), z: 16, core: 2. Of those that a mesh axis runs over, the one named last changes fastest.
Arguments:
- query_input: bfloat16 [65536, 2048], P(('seq', 'sub')), may hold values from -400 to 400
- key_input: bfloat16 [65536, 1024], P(('seq', 'sub')), may hold values from -400 to 400
- saved_value_input: bfloat16 [65536, 1024], P(('seq', 'sub')), may hold values from -6 to 6
- grad_output: bfloat16 [65536, 2048], P(('seq', 'sub')), may hold values from -16 to 16
- query_gain: float32 [128], replicated, may hold values from 0.5 to 1.5
- key_gain: float32 [128], replicated, may hold values from 0.5 to 1.5
Outputs:
- grad_query: bfloat16 [65536, 2048], P(('seq', 'sub'))
- grad_key: bfloat16 [65536, 1024], P(('seq', 'sub'))
- grad_value: bfloat16 [65536, 1024], P(('seq', 'sub'))
- grad_query_gain: float32 [128], replicated
- grad_key_gain: float32 [128], replicated
All inputs are finite; a program needn't handle non-finite values.
Results may differ from a plain program's by a relative error of at most 0.014.
Values may be sent and summed in bfloat16 or wider, within the bound.
A program may use at most 64 MiB of HBM per device.

v0:
```python
import jax
import jax.numpy as jnp
from jax import lax
from jax.sharding import PartitionSpec as P

WIN = 512


epsilon = 1e-06
score_scale = 168.0 ** (-0.5)


def shifted(array, axis, by):
    size = lax.axis_size(axis)
    pairs = [(i, i + by) for i in range(size) if 0 <= i + by < size]
    return lax.ppermute(array, axis, pairs)


def rope_tables(positions, half_width):
    frequency = 10000.0 ** (-jnp.arange(half_width).astype(jnp.float32) / half_width)
    angles = positions[:, None] * frequency[None, :]
    return (jnp.cos(angles), jnp.sin(angles))


def rotate(values, cosine_table, sine_table):
    half_width = values.shape[-1] // 2
    leading = values[..., :half_width]
    trailing = values[..., half_width:]
    cosine_wide = cosine_table[:, None, :]
    sine_wide = sine_table[:, None, :]
    return jnp.concatenate(
        [
            leading * cosine_wide - trailing * sine_wide,
            trailing * cosine_wide + leading * sine_wide,
        ],
        axis=-1,
    )


def prepare(raw_rows, gain_vector, cosine_table, sine_table):
    head_dim = gain_vector.shape[0]
    values = raw_rows.astype(jnp.float32).reshape(raw_rows.shape[0], -1, head_dim)
    inverse = lax.rsqrt(jnp.mean(values * values, axis=-1, keepdims=True) + epsilon)
    unit_rows = values * inverse
    prepared = rotate(unit_rows * gain_vector, cosine_table, sine_table).astype(jnp.bfloat16)
    return (prepared.reshape(raw_rows.shape), unit_rows, inverse)


def norm_back(grad_rotated, unit_rows, inverse, gain_vector, cosine_table, sine_table):
    grad_scaled = rotate(grad_rotated, cosine_table, -sine_table)
    gain_term = jnp.sum(grad_scaled * unit_rows, axis=(0, 1))
    grad_unit = grad_scaled * gain_vector
    grad_raw = (
        grad_unit - unit_rows * jnp.mean(grad_unit * unit_rows, axis=-1, keepdims=True)
    ) * inverse
    return (grad_raw.reshape(grad_raw.shape[0], -1).astype(jnp.bfloat16), gain_term)


def move_keys(payload, token_distance):
    return shifted(payload, ("seq", "sub"), token_distance)


def move_gradients(payload, token_distance):
    return shifted(payload, ("seq", "sub"), token_distance)


def per_device(query_input, key_input, saved_value_input, grad_output, query_gain, key_gain):
    first_row = lax.axis_index(("seq", "sub")) * query_input.shape[0]
    row_count = query_input.shape[0]
    halo_count = (WIN - 1) // row_count + 1
    head_dim = query_gain.shape[0]
    query_heads = query_input.shape[1] // head_dim
    key_heads = key_input.shape[1] // head_dim
    group_size = query_heads // key_heads
    pair_size = 2
    bundles = key_heads // pair_size
    key_span = (halo_count + 1) * row_count
    positions = (first_row + jnp.arange(row_count)).astype(jnp.float32)
    cosine_table, sine_table = rope_tables(positions, head_dim // 2)
    query_ready, query_unit, query_inverse = prepare(
        query_input, query_gain, cosine_table, sine_table
    )
    key_ready, key_unit, key_inverse = prepare(key_input, key_gain, cosine_table, sine_table)
    local_pair = jnp.stack([key_ready, saved_value_input])
    arrived = [move_keys(local_pair, token_distance) for token_distance in range(1, halo_count + 1)]
    key_pairs = jnp.concatenate(arrived[::-1] + [local_pair], axis=1)
    offsets_grid = (
        jnp.arange(row_count)[:, None] - jnp.arange(key_span)[None, :] + halo_count * row_count
    )
    key_positions = first_row - halo_count * row_count + jnp.arange(key_span)
    admitted = (offsets_grid >= 0) & (offsets_grid < WIN) & (key_positions[None, :] >= 0)
    query_bundles = jnp.moveaxis(
        query_ready.reshape(row_count, bundles, pair_size, group_size, head_dim), 1, 0
    )
    grad_bundles = jnp.moveaxis(
        grad_output.reshape(row_count, bundles, pair_size, group_size, head_dim), 1, 0
    )
    key_bundles = jnp.moveaxis(key_pairs[0].reshape(key_span, bundles, pair_size, head_dim), 1, 0)
    value_bundles = jnp.moveaxis(key_pairs[1].reshape(key_span, bundles, pair_size, head_dim), 1, 0)

    def attend_bundle(operands):
        queries, grads, key_rows, value_rows = operands
        scores = (
            jnp.einsum("ikgd,jkd->kgij", queries, key_rows, preferred_element_type=jnp.float32)
            * score_scale
        )
        weights = jnp.where(admitted, jnp.exp(scores), 0.0)
        probabilities = weights / jnp.sum(weights, axis=-1, keepdims=True)
        weights_low = probabilities.astype(jnp.bfloat16)
        grad_values = jnp.einsum(
            "kgij,ikgd->jkd", weights_low, grads, preferred_element_type=jnp.float32
        )
        grad_probs = jnp.einsum(
            "ikgd,jkd->kgij", grads, value_rows, preferred_element_type=jnp.float32
        )
        row_inner = jnp.sum(probabilities * grad_probs, axis=-1, keepdims=True)
        grad_scores = (probabilities * (grad_probs - row_inner) * score_scale).astype(jnp.bfloat16)
        grad_queries = jnp.einsum(
            "kgij,jkd->ikgd", grad_scores, key_rows, preferred_element_type=jnp.float32
        )
        grad_keys = jnp.einsum(
            "kgij,ikgd->jkd", grad_scores, queries, preferred_element_type=jnp.float32
        )
        return (grad_queries, grad_keys, grad_values)

    grad_queries, grad_keys, grad_values = lax.map(
        attend_bundle, (query_bundles, grad_bundles, key_bundles, value_bundles)
    )
    grad_query_rot = jnp.moveaxis(grad_queries, 0, 1).reshape(row_count, query_heads, head_dim)
    grad_key_all = jnp.moveaxis(grad_keys, 0, 1).reshape(key_span, key_heads * head_dim)
    grad_value_all = jnp.moveaxis(grad_values, 0, 1).reshape(key_span, key_heads * head_dim)
    grad_pairs = jnp.stack([grad_key_all, grad_value_all])
    grad_query_out, query_term = norm_back(
        grad_query_rot, query_unit, query_inverse, query_gain, cosine_table, sine_table
    )
    gathered_back = grad_pairs[:, halo_count * row_count :]
    for token_distance in range(1, halo_count + 1):
        slot_index = halo_count - token_distance
        outgoing = grad_pairs[:, slot_index * row_count : (slot_index + 1) * row_count]
        gathered_back = gathered_back + move_gradients(outgoing, -token_distance)
    grad_key_out, key_term = norm_back(
        gathered_back[0].reshape(row_count, key_heads, head_dim),
        key_unit,
        key_inverse,
        key_gain,
        cosine_table,
        sine_table,
    )
    grad_value_out = gathered_back[1].astype(jnp.bfloat16)
    query_total, key_total = lax.psum((query_term, key_term), ("seq", "sub"))
    return (grad_query_out, grad_key_out, grad_value_out, query_total, key_total)


def solution(mesh):
    in_specs = (
        P(("seq", "sub"), None),
        P(("seq", "sub"), None),
        P(("seq", "sub"), None),
        P(("seq", "sub"), None),
        P(),
        P(),
    )
    out_specs = (
        P(("seq", "sub"), None),
        P(("seq", "sub"), None),
        P(("seq", "sub"), None),
        P(),
        P(),
    )
    return jax.shard_map(
        per_device, mesh=mesh, in_specs=in_specs, out_specs=out_specs, check_vma=False
    )
```

profile of v0, /device:TPU:1, one launch (start us, length us, event | category | flops | bytes accessed | tf_op | source)
XLA Modules:
  0.0 329.2 jit_solution(16834727553455125497)
XLA Ops:
  4.5 6.4 %collective-permute-start = (bf16[2,128,1024]{1,2,0:T(8,128)(2,1)}, bf16[2,128,1024]{1,2,0:T(8,128)(2,1)}, u32[]{:S(2)}, u32[]{:S(2)}) collective-permute-start(bf16[2,128,1024]{1,2,0:T(8,128)(2,1)} %pad_maximum_fusion.2), channel_id=1, source_target_pairs={{0,4},{1,5},{2,6},{3,7},{4,8},{5,9},{6,10},{7,11},{8,12},{9,13},{1... | collective-permute-start | bytes 1572872 | tf_op jit(solution)/shard_map/ppermute | solution.py:16
  11.0 4.9 %collective-permute-start.1 = (bf16[2,128,1024]{1,2,0:T(8,128)(2,1)}, bf16[2,128,1024]{1,2,0:T(8,128)(2,1)}, u32[]{:S(2)}, u32[]{:S(2)}) collective-permute-start(bf16[2,128,1024]{1,2,0:T(8,128)(2,1)} %pad_maximum_fusion.2), channel_id=1, source_target_pairs={{0,3},{1,4},{2,5},{3,6},{4,7},{5,8},{6,9},{7,10},{8,11},{9,12},{10... | collective-permute-start | bytes 1572872 | tf_op jit(solution)/shard_map/ppermute | solution.py:16
  15.9 1.9 collective-permute-start.2
  17.8 3.8 %collective-permute-start.3 = (bf16[2,128,1024]{1,2,0:T(8,128)(2,1)}, bf16[2,128,1024]{1,2,0:T(8,128)(2,1)}, u32[]{:S(2)}, u32[]{:S(2)}) collective-permute-start(bf16[2,128,1024]{1,2,0:T(8,128)(2,1)} %pad_maximum_fusion.2), channel_id=1, source_target_pairs={{0,1},{1,2},{2,3},{3,4},{4,5},{5,6},{6,7},{7,8},{8,9},{9,10},{10,1... | collective-permute-start | bytes 1572872 | tf_op jit(solution)/shard_map/ppermute | solution.py:16
  28.3 5.3 %collective-permute-done.1 = bf16[2,128,1024]{1,2,0:T(8,128)(2,1)} collective-permute-done((bf16[2,128,1024]{1,2,0:T(8,128)(2,1)}, bf16[2,128,1024]{1,2,0:T(8,128)(2,1)}, u32[]{:S(2)}, u32[]{:S(2)}) %collective-permute-start.1) | collective-permute-done | bytes 524320 | tf_op jit(solution)/shard_map/ppermute | solution.py:16
  34.8 1.2 constant_dynamic-update-slice_fusion.2
  36.0 6.0 %collective-permute-done.3 = bf16[2,128,1024]{1,2,0:T(8,128)(2,1)} collective-permute-done((bf16[2,128,1024]{1,2,0:T(8,128)(2,1)}, bf16[2,128,1024]{1,2,0:T(8,128)(2,1)}, u32[]{:S(2)}, u32[]{:S(2)}) %collective-permute-start.3) | collective-permute-done | bytes 524320 | tf_op jit(solution)/shard_map/ppermute | solution.py:16
  43.3 1.3 fusion.85
  44.6 55.6 %while.15 = (s32[]{:T(128)}, f32[4,128,2,2,128]{1,4,3,2,0:T(8,128)}, f32[4,640,2,128]{1,3,2,0:T(8,128)}, f32[4,640,2,128]{1,3,2,0:T(8,128)}, bf16[4,640,2,128]{1...) while((s32[]{:T(128)}, ...), condition=%wide.region_5.6_spmd.clone, body=%wide.region_2.5_spmd.clone.sunk | while | flops 509383168 | bytes 20830948 | solution.py:126
  44.7 2.6 fusion.121
  47.4 1.3 convolution_bitcast_fusion.4
  48.7 3.2 fusion.123
  51.8 3.1 fusion.122
  54.9 1.4 fusion.124
  56.3 2.2 fusion.125
  58.7 2.6 fusion.121
  61.3 1.3 convolution_bitcast_fusion.4
  62.6 3.2 fusion.123
  65.8 3.0 fusion.122
  68.8 1.4 fusion.124
  70.2 2.2 fusion.125
  72.6 2.6 fusion.121
  75.2 1.3 convolution_bitcast_fusion.4
  76.5 3.2 fusion.123
  79.7 3.0 fusion.122
  82.6 1.4 fusion.124
  84.1 2.2 fusion.125
  86.4 2.6 fusion.121
  89.0 1.3 convolution_bitcast_fusion.4
  90.3 3.2 fusion.123
  93.6 3.0 fusion.122
  96.6 1.4 fusion.124
  98.0 2.2 fusion.125
  100.2 2.1 copy.95
  102.4 3.2 copy.96
  105.6 3.7 %fusion.71 = (f32[2,128,1024]{2,1,0:T(8,128)}, f32[2,128,1024]{2,1,0:T(8,128)}, f32[2,128,1024]{2,1,0:T(8,128)}, f32[2,128,1024]{2,1,0:T(8,128)}) fusion(f32[1,640,1024]{2,1,0:T(8,128)S(1)} %copy.95, f32[1,640,1024]{2,1,0:T(8,128)} %copy.96), kind=kLoop, calls=%fused_computation.73 | loop fusion | flops 1048576 | bytes 9437184 | tf_op jit(solution)/shard_map/stack | solution.py:132
  109.3 7.1 %collective-permute-start.4 = (f32[2,128,1024]{2,1,0:T(8,128)}, f32[2,128,1024]{2,1,0:T(8,128)}, u32[]{:S(2)}, u32[]{:S(2)}) collective-permute-start(f32[2,128,1024]{2,1,0:T(8,128)} %get-tuple-element.129), channel_id=1, source_target_pairs={{1,0},{2,1},{3,2},{4,3},{5,4},{6,5},{7,6},{8,7},{9,8},{10,9},{11,1... | collective-permute-start | bytes 3145736 | tf_op jit(solution)/shard_map/ppermute | solution.py:16
  116.4 1.9 collective-permute-start.5
  118.4 1.3 collective-permute-start.6
  119.7 1.5 collective-permute-start.7
  122.2 2.4 copy.102
  124.7 2.4 copy.103
  127.1 1.8 multiply_subtract_fusion
  130.9 2.2 fusion.77
  133.1 18.2 %collective-permute-done.4 = f32[2,128,1024]{2,1,0:T(8,128)} collective-permute-done((f32[2,128,1024]{2,1,0:T(8,128)}, f32[2,128,1024]{2,1,0:T(8,128)}, u32[]{:S(2)}, u32[]{:S(2)}) %collective-permute-start.4) | collective-permute-done | bytes 1048608 | tf_op jit(solution)/shard_map/ppermute | solution.py:16
  151.4 17.6 %collective-permute-done.6 = f32[2,128,1024]{2,1,0:T(8,128)} collective-permute-done((f32[2,128,1024]{2,1,0:T(8,128)}, f32[2,128,1024]{2,1,0:T(8,128)}, u32[]{:S(2)}, u32[]{:S(2)}) %collective-permute-start.6) | collective-permute-done | bytes 1048608 | tf_op jit(solution)/shard_map/ppermute | solution.py:16
  168.9 2.7 fusion.70
  174.9 154.3 %all-reduce = (f32[128]{0:T(128)}, f32[128]{0:T(128)}) all-reduce(f32[128]{0:T(128)S(1)} %bitcast_reduce_fusion, f32[128]{0:T(128)S(1)} %bitcast_reduce_fusion.1), channel_id=1, replica_groups=mesh['seq'=256,'sub'=2] {'seq','sub'}, use_global_device_ids=true, to_apply=%region_10.11 | all-reduce | flops 256 | bytes 2048 | tf_op jit(solution)/shard_map/psum | solution.py:150
  (79 shorter events, 19.6 us)
Async XLA Ops:
  0.7 1.7 copy-start.10
  2.6 1.0 copy-start.8
  2.8 18.8 %copy-start.3 = (bf16[128,2048]{1,0:T(8,128)(2,1)S(1)}, bf16[128,2048]{1,0:T(8,128)(2,1)}, u32[]{:S(2)}) copy-start(bf16[128,2048]{1,0:T(8,128)(2,1)} %param.8) | copy-start | bytes 1572868
  4.5 22.6 %collective-permute-start = (bf16[2,128,1024]{1,2,0:T(8,128)(2,1)}, bf16[2,128,1024]{1,2,0:T(8,128)(2,1)}, u32[]{:S(2)}, u32[]{:S(2)}) collective-permute-start(bf16[2,128,1024]{1,2,0:T(8,128)(2,1)} %pad_maximum_fusion.2), channel_id=1, source_target_pairs={{0,4},{1,5},{2,6},{3,7},{4,8},{5,9},{6,10},{7,11},{8,12},{9,13},{1... | collective-permute-start | bytes 1572872 | tf_op jit(solution)/shard_map/ppermute | solution.py:16
  11.0 22.6 %collective-permute-start.1 = (bf16[2,128,1024]{1,2,0:T(8,128)(2,1)}, bf16[2,128,1024]{1,2,0:T(8,128)(2,1)}, u32[]{:S(2)}, u32[]{:S(2)}) collective-permute-start(bf16[2,128,1024]{1,2,0:T(8,128)(2,1)} %pad_maximum_fusion.2), channel_id=1, source_target_pairs={{0,3},{1,4},{2,5},{3,6},{4,7},{5,8},{6,9},{7,10},{8,11},{9,12},{10... | collective-permute-start | bytes 1572872 | tf_op jit(solution)/shard_map/ppermute | solution.py:16
  15.9 18.9 %collective-permute-start.2 = (bf16[2,128,1024]{1,2,0:T(8,128)(2,1)}, bf16[2,128,1024]{1,2,0:T(8,128)(2,1)}, u32[]{:S(2)}, u32[]{:S(2)}) collective-permute-start(bf16[2,128,1024]{1,2,0:T(8,128)(2,1)} %pad_maximum_fusion.2), channel_id=1, source_target_pairs={{0,2},{1,3},{2,4},{3,5},{4,6},{5,7},{6,8},{7,9},{8,10},{9,11},{10,... | collective-permute-start | bytes 1572872 | tf_op jit(solution)/shard_map/ppermute | solution.py:16
  17.8 24.2 %collective-permute-start.3 = (bf16[2,128,1024]{1,2,0:T(8,128)(2,1)}, bf16[2,128,1024]{1,2,0:T(8,128)(2,1)}, u32[]{:S(2)}, u32[]{:S(2)}) collective-permute-start(bf16[2,128,1024]{1,2,0:T(8,128)(2,1)} %pad_maximum_fusion.2), channel_id=1, source_target_pairs={{0,1},{1,2},{2,3},{3,4},{4,5},{5,6},{6,7},{7,8},{8,9},{9,10},{10,1... | collective-permute-start | bytes 1572872 | tf_op jit(solution)/shard_map/ppermute | solution.py:16
  21.8 1.3 copy-start.9
  22.0 1.1 copy-start.1
  23.9 1.0 copy-start.7
  105.6 15.5 %copy-start.5 = (f32[4,128,2,2,128]{1,4,3,2,0:T(8,128)S(1)}, f32[4,128,2,2,128]{1,4,3,2,0:T(8,128)}, u32[]{:S(2)}) copy-start(f32[4,128,2,2,128]{1,4,3,2,0:T(8,128)} %get-tuple-element.54) | copy-start | bytes 3145732
  109.3 42.1 %collective-permute-start.4 = (f32[2,128,1024]{2,1,0:T(8,128)}, f32[2,128,1024]{2,1,0:T(8,128)}, u32[]{:S(2)}, u32[]{:S(2)}) collective-permute-start(f32[2,128,1024]{2,1,0:T(8,128)} %get-tuple-element.129), channel_id=1, source_target_pairs={{1,0},{2,1},{3,2},{4,3},{5,4},{6,5},{7,6},{8,7},{9,8},{10,9},{11,1... | collective-permute-start | bytes 3145736 | tf_op jit(solution)/shard_map/ppermute | solution.py:16
  116.4 34.9 %collective-permute-start.5 = (f32[2,128,1024]{2,1,0:T(8,128)}, f32[2,128,1024]{2,1,0:T(8,128)}, u32[]{:S(2)}, u32[]{:S(2)}) collective-permute-start(f32[2,128,1024]{2,1,0:T(8,128)} %get-tuple-element.130), channel_id=1, source_target_pairs={{2,0},{3,1},{4,2},{5,3},{6,4},{7,5},{8,6},{9,7},{10,8},{11,9},{12,... | collective-permute-start | bytes 3145736 | tf_op jit(solution)/shard_map/ppermute | solution.py:16
  118.4 50.6 %collective-permute-start.6 = (f32[2,128,1024]{2,1,0:T(8,128)}, f32[2,128,1024]{2,1,0:T(8,128)}, u32[]{:S(2)}, u32[]{:S(2)}) collective-permute-start(f32[2,128,1024]{2,1,0:T(8,128)} %get-tuple-element.132), channel_id=1, source_target_pairs={{3,0},{4,1},{5,2},{6,3},{7,4},{8,5},{9,6},{10,7},{11,8},{12,9},{13... | collective-permute-start | bytes 3145736 | tf_op jit(solution)/shard_map/ppermute | solution.py:16
  119.7 49.3 %collective-permute-start.7 = (f32[2,128,1024]{2,1,0:T(8,128)}, f32[2,128,1024]{2,1,0:T(8,128)}, u32[]{:S(2)}, u32[]{:S(2)}) collective-permute-start(f32[2,128,1024]{2,1,0:T(8,128)} %get-tuple-element.131), channel_id=1, source_target_pairs={{4,0},{5,1},{6,2},{7,3},{8,4},{9,5},{10,6},{11,7},{12,8},{13,9},{1... | collective-permute-start | bytes 3145736 | tf_op jit(solution)/shard_map/ppermute | solution.py:16
  127.1 1.9 copy-start.2
  129.9 1.0 copy-start.4
  130.9 38.0 %copy-start = (f32[1,640,1024]{2,1,0:T(8,128)S(1)}, f32[1,640,1024]{2,1,0:T(8,128)}, u32[]{:S(2)}) copy-start(f32[1,640,1024]{2,1,0:T(8,128)} %copy.96) | copy-start | bytes 7864324
  172.8 1.0 copy-start.6
where the time goes:
time: 331 us; the launch traced here: 329 us
  blocking collectives  154 us (47%)
  matrix products  54.9 us (17%)
  waiting for transfers between devices  47.1 us (14%)
  starting transfers between devices  28.9 us (9%)
  local copies, waits for them, and re-layouts  23.2 us (7%)
  other arithmetic  19.5 us (6%)
    psum x1, blocking collectives, per_device(): query_total, key_total = lax.psum((query_term, key_term), ('seq', 'sub'))  154 us
    ppermute x8, waiting for transfers between devices, shifted(): return lax.ppermute(array, axis, pairs)  47.1 us
    ppermute x8, starting transfers between devices, shifted(): return lax.ppermute(array, axis, pairs)  28.9 us
    unnamed x34, local copies, waits for them, and re-layouts  13.1 us
    dot_general x4, matrix products, attend_bundle(): jnp.einsum('kgij,ikgd->jkd', grad_scores, queries, preferred_element_type...  12.7 us
    dot_general x4, matrix products, attend_bundle(): jnp.einsum('kgij,jkd->ikgd', grad_scores, key_rows, preferred_element_typ...  12.1 us
    div x4, matrix products, attend_bundle(): probabilities = weights / jnp.sum(weights, axis=-1, keepdims=True)  10.5 us
    dot_general x4, matrix products, attend_bundle(): jnp.einsum('kgij,ikgd->jkd', weights_low, grads, preferred_element_type=j...  8.79 us
  transfers between devices with their start and end apart: 8, of which 4 were waited for; matrix products, arithmetic and copies ran while one was open for 6% of the time, Pallas kernels for 0%

commit v1 on v0

v1 whole, which is shorter than its diff:
```python
import functools

import jax
import jax.numpy as jnp
import numpy as np
from jax import lax
from jax.experimental import pallas as pl
from jax.experimental.pallas import tpu as pltpu
from jax.sharding import PartitionSpec as P

MESH = pl.DeviceIdType.MESH
T = 128
D = 128
NP = 8
NH = 4
NZ = 16
NX = 4
EPS = 1e-6
SCALE = 168.0 ** (-0.5)
LOG2E = 1.4426950408889634
LN2 = 0.6931471805599453
F32 = jnp.float32
BF16 = jnp.bfloat16


def device(col, y, c):
    return ((col * 2 + y // 2) * 2 + c, y % 2)


def place(y, c):
    return 4 * (y // 2) + 2 * c + y % 2


def rows_of(block):
    return pl.ds(pl.multiple_of(block * T, T), T)


def cols_of(start, size):
    return pl.ds(pl.multiple_of(start, 128), size)


def unit_of(raw):
    inverse = lax.rsqrt(jnp.mean(raw * raw, axis=-1, keepdims=True) + EPS)
    return raw * inverse, inverse


def rope(rows, cosine, sine):
    return rows * cosine + pltpu.roll(rows, 64, 1) * sine


def rope_back(rows, cosine, sine):
    return rows * cosine - pltpu.roll(rows, 64, 1) * sine


def dot_nt(a, b):
    return lax.dot_general(a, b, (((1,), (1,)), ((), ())), preferred_element_type=F32)


def dot_nn(a, b):
    return jnp.dot(a, b, preferred_element_type=F32)


def kernel(
    q_in,
    k_in,
    v_in,
    g_in,
    qgain_ref,
    kgain_ref,
    freq_ref,
    dq_out,
    dk_out,
    dv_out,
    qterm_out,
    kterm_out,
    st_kv,
    st_qg,
    kv,
    qg,
    kready,
    ktrans,
    ctab,
    stab,
    weights,
    gprobs,
    dkv,
    dq_res,
    dkv_res,
    halo_res,
    halo_ret,
    plane_q,
    plane_kv,
    terms,
    ar_a,
    ar_b,
    ar_c,
    core_send,
    core_recv,
    kv_send,
    kv_recv,
    qg_send,
    qg_recv,
    halo_send,
    halo_recv,
    ret_send,
    ret_recv,
    dq_send,
    dq_recv,
    dkv_send,
    dkv_recv,
    out_send,
    out_recv,
    out_local,
    ara_send,
    ara_recv,
    arb_send,
    arb_recv,
    arc_send,
    arc_recv,
):
    s = lax.axis_index("seq")
    c = s % 2
    col = s // 4
    y = 2 * ((s // 2) % 2) + lax.axis_index("sub")
    z = col % NZ
    x = col // NZ
    other = 1 - c
    mine = place(y, c)
    theirs = place(y, other)
    partner = device(col, y, other)
    after = device((col + 1) % (NX * NZ), y, c)
    before = device((col + NX * NZ - 1) % (NX * NZ), y, c)

    column_peers = [(dy, dc) for dy in range(4) for dc in range(2) if (dy, dc) != (0, 0)]

    def column_device(dy, dc):
        return device(col, (y + dy) % 4, (c + dc) % 2)

    def z_device(dz):
        return device(x * NZ + (z + dz) % NZ, y, c)

    def x_device(dx):
        return device(((x + dx) % NX) * NZ + z, y, c)

    barrier = pltpu.get_barrier_semaphore()
    greeted = [column_device(dy, dc) for dy, dc in column_peers]
    greeted += [after, before]
    greeted += [z_device(dz) for dz in range(1, NZ)]
    greeted += [x_device(dx) for dx in range(1, NX)]
    for target in greeted:
        pl.semaphore_signal(barrier, inc=1, device_id=target, device_id_type=MESH)
    pl.semaphore_wait(barrier, len(greeted))

    def remote(src, dst, send, recv, target):
        return pltpu.make_async_remote_copy(
            src_ref=src, dst_ref=dst, send_sem=send, recv_sem=recv, device_id=target, device_id_type=MESH
        )

    sends = []

    core_copies = []
    for i, (ref, width) in enumerate(((k_in, 4 * D), (v_in, 4 * D), (q_in, 8 * D), (g_in, 8 * D))):
        stage = st_kv.at[i] if i < 2 else st_qg.at[i - 2]
        core_copies.append(
            remote(ref.at[:, cols_of(other * width, width)], stage, core_send.at[i], core_recv.at[i], partner)
        )

    def spread(kind, sources, width, slots, first_row_block, send, recv, block, turn):
        for i, source in enumerate(sources):
            base, ref = source
            for dy in range(1, 4):
                yy = (y + dy) % 4
                copy = remote(
                    ref.at[:, cols_of(base + yy * width, width)],
                    slots.at[i, rows_of(first_row_block + block)],
                    send.at[turn, i, dy],
                    recv.at[i, block],
                    device(col, yy, c),
                )
                copy.start()
                sends.append(copy)
            pltpu.make_async_copy(
                ref.at[:, cols_of(base + y * width, width)],
                slots.at[i, rows_of(first_row_block + block)],
                recv.at[i, block],
            ).start()

    core_copies[0].start()
    core_copies[1].start()
    own_kv = [(c * 4 * D, k_in), (c * 4 * D, v_in)]
    spread("kv", own_kv, D, kv, NH, kv_send, kv_recv, mine, 0)
    core_copies[2].start()
    core_copies[3].start()
    core_copies[0].wait_recv()
    core_copies[1].wait_recv()
    spread("kv", [(0, st_kv.at[0]), (0, st_kv.at[1])], D, kv, NH, kv_send, kv_recv, theirs, 1)
    own_qg = [(c * 8 * D, q_in), (c * 8 * D, g_in)]
    spread("qg", own_qg, 2 * D, qg, 0, qg_send, qg_recv, mine, 0)
    core_copies[2].wait_recv()
    core_copies[3].wait_recv()
    spread("qg", [(0, st_qg.at[0]), (0, st_qg.at[1])], 2 * D, qg, 0, qg_send, qg_recv, theirs, 1)

    first_token = col * (NP * T) - NH * T
    half = (NP + NH) * T // 2
    step_rows = 64

    @pl.loop(0, half // step_rows)
    def _(step):
        row = lax.broadcasted_iota(jnp.int32, (step_rows, D), 0)
        lane = lax.broadcasted_iota(jnp.int32, (step_rows, D), 1)
        low = lane < 64
        token = first_token + step * step_rows + row + jnp.where(low, 0, half)
        angle = token.astype(F32) * freq_ref[...]
        cosine = jnp.cos(angle)
        sine = jnp.sin(angle)
        cosine_turned = pltpu.roll(cosine, 64, 1)
        sine_turned = pltpu.roll(sine, 64, 1)
        near = pl.ds(pl.multiple_of(step * step_rows, step_rows), step_rows)
        far = pl.ds(pl.multiple_of(half + step * step_rows, step_rows), step_rows)
        ctab[near] = jnp.where(low, cosine, cosine_turned)
        ctab[far] = jnp.where(low, cosine_turned, cosine)
        stab[near] = jnp.where(low, -sine, sine_turned)
        stab[far] = jnp.where(low, -sine_turned, sine)

    dkv[...] = jnp.zeros_like(dkv)
    terms[...] = jnp.zeros_like(terms)
    kgain = kgain_ref[...]
    qgain = qgain_ref[...]

    def wait_kv(block):
        for i in range(2):
            slot = kv.at[i, rows_of(NH + block)]
            pltpu.make_async_copy(slot, slot, kv_recv.at[i, block]).wait()

    def halo_copy(i):
        return remote(
            kv.at[:, rows_of(NP + i)], kv.at[:, rows_of(i)], halo_send.at[i], halo_recv.at[i], after
        )

    def prepare_keys(block):
        rows = rows_of(block)
        unit, _ = unit_of(kv[0, rows].astype(F32))
        turned = rope(unit * kgain, ctab[rows], stab[rows])
        kready[rows] = turned.astype(BF16)
        ktrans[block] = turned.T.astype(BF16)

    @pl.loop(0, NH)
    def _(i):
        wait_kv(NH + i)
        halo_copy(i).start()

    @pl.loop(0, NH)
    def _(i):
        wait_kv(i)

    @pl.loop(NH, NH + NP)
    def _(block):
        prepare_keys(block)

    halo_valid = jnp.where(col == 0, 0.0, 1.0)
    key_row = lax.broadcasted_iota(jnp.int32, (T, 2 * T), 0)
    query_lane = lax.broadcasted_iota(jnp.int32, (T, 2 * T), 1) % T
    newer = key_row > query_lane

    def norm_back(turned_grad, raw, gain, cosine, sine):
        unit, inverse = unit_of(raw)
        w = rope_back(turned_grad, cosine, sine)
        term = jnp.sum(w * unit, axis=0, keepdims=True)
        grad_unit = w * gain
        grad = (grad_unit - unit * jnp.mean(grad_unit * unit, axis=-1, keepdims=True)) * inverse
        return grad.astype(BF16), term

    def owner(block):
        return 2 * (block // 4) + block % 2, (block // 2) % 2

    def dq_copies(block):
        yy, cc = owner(block)
        src = dq_res.at[block]
        dst = plane_q.at[cc, :, cols_of(y * 2 * D, 2 * D)]
        return (
            remote(src, dst, dq_send.at[block], dq_recv.at[y, cc], device(col, yy, c)),
            pltpu.make_async_copy(src, dst, dq_recv.at[y, cc]),
            yy,
        )

    def dkv_copies(block):
        yy, cc = owner(block)
        src = dkv_res.at[block]
        dst = plane_kv.at[cc, :, :, cols_of(y * D, D)]
        return (
            remote(src, dst, dkv_send.at[block], dkv_recv.at[y, cc], device(col, yy, c)),
            pltpu.make_async_copy(src, dst, dkv_recv.at[y, cc]),
            yy,
        )

    def give(copies):
        far, near, yy = copies

        @pl.when(yy == y)
        def _():
            near.start()

        @pl.when(yy != y)
        def _():
            far.start()

    def attend(block):
        rows = rows_of(block)
        for i in range(2):
            slot = qg.at[i, rows]
            pltpu.make_async_copy(slot, slot, qg_recv.at[i, block]).wait()
        own = rows_of(block + NH)
        cosine, sine = ctab[own], stab[own]
        raw = [qg[0, rows, h * D : (h + 1) * D].astype(F32) for h in range(2)]
        queries = jnp.concatenate(
            [(rope(unit_of(r)[0] * qgain, cosine, sine) * (SCALE * LOG2E)).astype(BF16) for r in raw], axis=0
        )
        grads = jnp.concatenate([qg[1, rows, h * D : (h + 1) * D] for h in range(2)], axis=0)
        total = jnp.zeros((1, 2 * T), F32)
        inner = jnp.zeros((1, 2 * T), F32)
        for t in range(NH + 1):
            keys = rows_of(block + t)
            weight = jnp.exp2(dot_nt(kready[keys], queries))
            if t == 0:
                weight = jnp.where(newer, weight, 0.0)
            if t == NH:
                weight = jnp.where(newer, 0.0, weight)
            else:
                weight = weight * jnp.where(block + t < NH, halo_valid, 1.0)
            grad_prob = dot_nt(kv[1, keys], grads)
            total = total + jnp.sum(weight, axis=0, keepdims=True)
            inner = inner + jnp.sum(weight * grad_prob, axis=0, keepdims=True)
            weights[t] = weight
            gprobs[t] = grad_prob
        inverse = 1.0 / total
        inner = inner * inverse
        grad_query = jnp.zeros((D, 2 * T), F32)
        for t in range(NH + 1):
            keys = rows_of(block + t)
            prob = weights[t] * inverse
            grad_score = (prob * (gprobs[t] - inner)).astype(BF16)
            dkv[1, keys] += dot_nn(prob.astype(BF16), grads)
            dkv[0, keys] += dot_nn(grad_score, queries)
            grad_query = grad_query + dot_nn(ktrans[block + t], grad_score)
        for h in range(2):
            turned = grad_query[:, h * T : (h + 1) * T].T * SCALE
            grad, term = norm_back(turned, raw[h], qgain, cosine, sine)
            dq_res[block, :, h * D : (h + 1) * D] = grad
            terms[0:1] += term
        give(dq_copies(block))

    @pl.loop(NH, NP)
    def _(block):
        attend(block)

    @pl.loop(0, NH)
    def _(i):
        halo_copy(i).wait_recv()
        prepare_keys(i)

    def return_copy(i):
        return remote(halo_res.at[i], halo_ret.at[i], ret_send.at[i], ret_recv.at[i], before)

    @pl.loop(0, NH)
    def _(block):
        attend(block)
        keys = rows_of(block)
        grad_key = dkv[0, keys] * LN2
        halo_res[block, 0] = grad_key.astype(BF16)
        halo_res[block, 1] = dkv[1, keys].astype(BF16)
        return_copy(block).start()
        unit, _ = unit_of(kv[0, keys].astype(F32))
        w = rope_back(grad_key, ctab[keys], stab[keys])
        terms[1:2] += jnp.sum(w * unit, axis=0, keepdims=True)

    @pl.loop(0, NH)
    def _(block):
        keys = rows_of(block + NH)
        grad, term = norm_back(dkv[0, keys] * LN2, kv[0, keys].astype(F32), kgain, ctab[keys], stab[keys])
        dkv_res[block, 0] = grad
        dkv_res[block, 1] = dkv[1, keys].astype(BF16)
        terms[1:2] += term
        give(dkv_copies(block))

    @pl.loop(NH, NP)
    def _(block):
        keys = rows_of(block + NH)
        unit, _ = unit_of(kv[0, keys].astype(F32))
        w = rope_back(dkv[0, keys] * LN2, ctab[keys], stab[keys])
        terms[1:2] += jnp.sum(w * unit, axis=0, keepdims=True)

    ar_a[mine] = terms[...]
    stage_a = [
        remote(terms, ar_a.at[mine], ara_send.at[i], ara_recv.at[mine], column_device(dy, dc))
        for i, (dy, dc) in enumerate(column_peers)
    ]
    for copy in stage_a:
        copy.start()
    for dy, dc in column_peers:
        slot = place((y + dy) % 4, (c + dc) % 2)
        pltpu.make_async_copy(ar_a.at[slot], ar_a.at[slot], ara_recv.at[slot]).wait()
    ar_b[z] = jnp.sum(ar_a[...], axis=0)
    stage_b = [
        remote(ar_b.at[z], ar_b.at[z], arb_send.at[dz], arb_recv.at[z], z_device(dz)) for dz in range(1, NZ)
    ]
    for copy in stage_b:
        copy.start()
    for dz in range(1, NZ):
        slot = (z + dz) % NZ
        pltpu.make_async_copy(ar_b.at[slot], ar_b.at[slot], arb_recv.at[slot]).wait()
    ar_c[x] = jnp.sum(ar_b[...], axis=0)
    stage_c = [
        remote(ar_c.at[x], ar_c.at[x], arc_send.at[dx], arc_recv.at[x], x_device(dx)) for dx in range(1, NX)
    ]
    for copy in stage_c:
        copy.start()

    @pl.loop(NH, NP)
    def _(block):
        return_copy(block - NH).wait_recv()
        keys = rows_of(block + NH)
        grad_key = dkv[0, keys] * LN2 + halo_ret[block - NH, 0].astype(F32)
        grad, _ = norm_back(grad_key, kv[0, keys].astype(F32), kgain, ctab[keys], stab[keys])
        dkv_res[block, 0] = grad
        dkv_res[block, 1] = (dkv[1, keys] + halo_ret[block - NH, 1].astype(F32)).astype(BF16)
        give(dkv_copies(block))

    wide, narrow = cols_of(c * 8 * D, 8 * D), cols_of(c * 4 * D, 4 * D)
    plane_parts = (
        (lambda cc: plane_q.at[cc], dq_out.at[:, wide]),
        (lambda cc: plane_kv.at[cc, 0], dk_out.at[:, narrow]),
        (lambda cc: plane_kv.at[cc, 1], dv_out.at[:, narrow]),
    )
    out_copies = []
    for i, (part, target) in enumerate(plane_parts):
        if i < 2:
            for cc in range(2):
                for yy in range(4):
                    if i == 0:
                        slot = plane_q.at[cc, :, cols_of(yy * 2 * D, 2 * D)]
                        sem = dq_recv.at[yy, cc]
                    else:
                        slot = plane_kv.at[cc, :, :, cols_of(yy * D, D)]
                        sem = dkv_recv.at[yy, cc]
                    pltpu.make_async_copy(slot, slot, sem).wait()
        away = remote(part(other), target, out_send.at[i], out_recv.at[i], partner)
        stay = pltpu.make_async_copy(part(c), target, out_local.at[i])
        away.start()
        stay.start()
        out_copies.append((away, stay))

    for dx in range(1, NX):
        slot = (x + dx) % NX
        pltpu.make_async_copy(ar_c.at[slot], ar_c.at[slot], arc_recv.at[slot]).wait()
    gains = jnp.sum(ar_c[...], axis=0)
    qterm_out[...] = gains[0:1]
    kterm_out[...] = gains[1:2]

    for copy in core_copies + sends + stage_a + stage_b + stage_c:
        copy.wait_send()

    @pl.loop(0, NH)
    def _(i):
        halo_copy(i).wait_send()
        return_copy(i).wait_send()

    @pl.loop(0, NP)
    def _(block):
        yy, _ = owner(block)

        @pl.when(yy != y)
        def _():
            dq_copies(block)[0].wait_send()
            dkv_copies(block)[0].wait_send()

    for away, stay in out_copies:
        away.wait()
        stay.wait()


def per_device(query_input, key_input, saved_value_input, grad_output, query_gain, key_gain):
    frequency = (10000.0 ** (-np.arange(64, dtype=np.float64) / 64)).astype(np.float32)
    frequency = jnp.asarray(np.concatenate([frequency, frequency])[None, :])
    anywhere = pl.BlockSpec(memory_space=pl.ANY)
    vmem = pl.BlockSpec(memory_space=pltpu.VMEM)
    dma = pltpu.SemaphoreType.DMA
    span = (NP + NH) * T
    dq, dk, dv, qterm, kterm = pl.pallas_call(
        kernel,
        out_shape=(
            jax.ShapeDtypeStruct((T, 16 * D), BF16),
            jax.ShapeDtypeStruct((T, 8 * D), BF16),
            jax.ShapeDtypeStruct((T, 8 * D), BF16),
            jax.ShapeDtypeStruct((1, D), F32),
            jax.ShapeDtypeStruct((1, D), F32),
        ),
        in_specs=[anywhere] * 4 + [vmem] * 3,
        out_specs=(anywhere, anywhere, anywhere, vmem, vmem),
        scratch_shapes=[
            pltpu.VMEM((2, T, 4 * D), BF16),
            pltpu.VMEM((2, T, 8 * D), BF16),
            pltpu.VMEM((2, span, D), BF16),
            pltpu.VMEM((2, NP * T, 2 * D), BF16),
            pltpu.VMEM((span, D), BF16),
            pltpu.VMEM((NP + NH, D, T), BF16),
            pltpu.VMEM((span, D), F32),
            pltpu.VMEM((span, D), F32),
            pltpu.VMEM((NH + 1, T, 2 * T), F32),
            pltpu.VMEM((NH + 1, T, 2 * T), F32),
            pltpu.VMEM((2, span, D), F32),
            pltpu.VMEM((NP, T, 2 * D), BF16),
            pltpu.VMEM((NP, 2, T, D), BF16),
            pltpu.VMEM((NH, 2, T, D), BF16),
            pltpu.VMEM((NH, 2, T, D), BF16),
            pltpu.VMEM((2, T, 8 * D), BF16),
            pltpu.VMEM((2, 2, T, 4 * D), BF16),
            pltpu.VMEM((8, D), F32),
            pltpu.VMEM((NP, 8, D), F32),
            pltpu.VMEM((NZ, 8, D), F32),
            pltpu.VMEM((NX, 8, D), F32),
            dma((4,)),
            dma((4,)),
            dma((2, 2, 4)),
            dma((2, NP)),
            dma((2, 2, 4)),
            dma((2, NP)),
            dma((NH,)),
            dma((NH,)),
            dma((NH,)),
            dma((NH,)),
            dma((NP,)),
            dma((4, 2)),
            dma((NP,)),
            dma((4, 2)),
            dma((3,)),
            dma((3,)),
            dma((3,)),
            dma((NP,)),
            dma((NP,)),
            dma((NZ,)),
            dma((NZ,)),
            dma((NX,)),
            dma((NX,)),
        ],
        compiler_params=pltpu.CompilerParams(
            collective_id=0, has_side_effects=True, vmem_limit_bytes=40 * 2**20
        ),
        cost_estimate=pl.CostEstimate(flops=1700000000, bytes_accessed=3000000, transcendentals=1400000),
    )(
        query_input,
        key_input,
        saved_value_input,
        grad_output,
        query_gain.reshape(1, D),
        key_gain.reshape(1, D),
        frequency,
    )
    return dq, dk, dv, qterm.reshape(D), kterm.reshape(D)


def solution(mesh):
    tokens = P(("seq", "sub"), None)
    return jax.shard_map(
        per_device,
        mesh=mesh,
        in_specs=(tokens, tokens, tokens, tokens, P(), P()),
        out_specs=(tokens, tokens, tokens, P(), P()),
        check_vma=False,
    )
```

time: 331 us -> 77.4 us (0.23)
  the two profiles are of different devices: /device:TPU:1 before, /device:TPU:27 now
where the time goes in v1:
time: 77.4 us; the launch traced here: 77.1 us
  Pallas kernels  68.5 us (89%)
  local copies, waits for them, and re-layouts  7.87 us (10%)
    pallas_call x1, Pallas kernels, per_device(): pl.pallas_call(kernel, out_shape=(jax.ShapeDtypeStruct((T, 16 * D), BF16)...  68.5 us
    unnamed x19, local copies, waits for them, and re-layouts  7.87 us

profile of v1, /device:TPU:27, one launch (start us, length us, event | category | flops | bytes accessed | tf_op | source)
XLA Modules:
  0.0 77.1 jit_solution(2086341477948025919)
XLA Ops:
  0.6 0.0 copy-start.4
  0.6 0.0 copy-start.5
  0.7 0.0 copy-start.6
  0.7 0.6 copy-done.4
  1.3 0.0 copy-done.5
  1.3 0.0 copy-done.6
  1.3 0.0 copy-start
  1.3 1.0 %copy-done = bf16[128,2048]{1,0:T(8,128)(2,1)S(1)} copy-done((bf16[128,2048]{1,0:T(8,128)(2,1)S(1)}, bf16[128,2048]{1,0:T(8,128)(2,1)}, u32[]{:S(2)}) %copy-start) | copy-done | bytes 524312
  2.4 0.0 copy-start.1
  2.4 1.0 %copy-done.1 = bf16[128,2048]{1,0:T(8,128)(2,1)S(1)} copy-done((bf16[128,2048]{1,0:T(8,128)(2,1)S(1)}, bf16[128,2048]{1,0:T(8,128)(2,1)}, u32[]{:S(2)}) %copy-start.1) | copy-done | bytes 524312
  3.4 0.0 copy-start.2
  3.4 0.9 %copy-done.2 = bf16[128,1024]{1,0:T(8,128)(2,1)S(1)} copy-done((bf16[128,1024]{1,0:T(8,128)(2,1)S(1)}, bf16[128,1024]{1,0:T(8,128)(2,1)}, u32[]{:S(2)}) %copy-start.2) | copy-done | bytes 262168
  4.4 0.0 copy-start.3
  4.4 0.9 %copy-done.3 = bf16[128,1024]{1,0:T(8,128)(2,1)S(1)} copy-done((bf16[128,1024]{1,0:T(8,128)(2,1)S(1)}, bf16[128,1024]{1,0:T(8,128)(2,1)}, u32[]{:S(2)}) %copy-start.3) | copy-done | bytes 262168
  5.3 68.5 %shard_map.110 = (bf16[128,2048]{1,0:T(8,128)(2,1)S(1)}, bf16[128,1024]{1,0:T(8,128)(2,1)S(1)}, bf16[128,1024]{1,0:T(8,128)(2,1)S(1)}, f32[1,128]{1,0:T(1,128)S(1)}, f32[1,128]{1,0:T(1,128)S(1)}) custom-call(bf16[128,2048]{1,0:T(8,128)(2,1)S(1)} %copy-done, bf16[128,1024]{1,0:T(8,128)(2,1)S(1)} %copy-done.2, bf16[128,1024]{1,0:T(8,128)(2,1)S(1)} %copy-done.3, ...), custom_call_target="tpu_custom_call" | custom-call | flops 1700000000 | bytes 3000000 | tf_op jit(solution)/shard_map/pallas_call | solution.py:488
  73.9 0.8 %copy.17 = bf16[128,2048]{1,0:T(8,128)(2,1)} copy(bf16[128,2048]{1,0:T(8,128)(2,1)S(1)} %get-tuple-element.20) | data formatting | bytes 1048576
  74.7 0.7 copy.18
  75.4 0.7 copy.19
  76.1 0.5 copy.20
  76.6 0.5 copy.21
Async XLA Ops:
  0.6 0.7 copy-start.4
  0.6 0.7 copy-start.5
  0.7 0.7 copy-start.6
  1.3 1.0 %copy-start = (bf16[128,2048]{1,0:T(8,128)(2,1)S(1)}, bf16[128,2048]{1,0:T(8,128)(2,1)}, u32[]{:S(2)}) copy-start(bf16[128,2048]{1,0:T(8,128)(2,1)} %q_in.1) | copy-start | bytes 1572868
  2.4 1.0 %copy-start.1 = (bf16[128,2048]{1,0:T(8,128)(2,1)S(1)}, bf16[128,2048]{1,0:T(8,128)(2,1)}, u32[]{:S(2)}) copy-start(bf16[128,2048]{1,0:T(8,128)(2,1)} %g_in.1) | copy-start | bytes 1572868
  3.4 0.9 %copy-start.2 = (bf16[128,1024]{1,0:T(8,128)(2,1)S(1)}, bf16[128,1024]{1,0:T(8,128)(2,1)}, u32[]{:S(2)}) copy-start(bf16[128,1024]{1,0:T(8,128)(2,1)} %k_in.1) | copy-start | bytes 786436
  4.4 0.9 %copy-start.3 = (bf16[128,1024]{1,0:T(8,128)(2,1)S(1)}, bf16[128,1024]{1,0:T(8,128)(2,1)}, u32[]{:S(2)}) copy-start(bf16[128,1024]{1,0:T(8,128)(2,1)} %v_in.1) | copy-start | bytes 786436

commit v2 on v1

--- a/solution.py
+++ b/solution.py
@@ -65,14 +65,17 @@
     k_in,
     v_in,
     g_in,
-    qgain_ref,
-    kgain_ref,
-    freq_ref,
+    qgain_in,
+    kgain_in,
+    freq_in,
     dq_out,
     dk_out,
     dv_out,
     qterm_out,
     kterm_out,
+    qgain_ref,
+    kgain_ref,
+    freq_ref,
     st_kv,
     st_qg,
     kv,
@@ -117,6 +120,11 @@
     arb_recv,
     arc_send,
     arc_recv,
+    small_sem,
+    relay_up,
+    relay_one,
+    relay_two,
+    relay_four,
 ):
     s = lax.axis_index("seq")
     c = s % 2
@@ -142,14 +150,24 @@
     def x_device(dx):
         return device(((x + dx) % NX) * NZ + z, y, c)
 
+    def greet(semaphore, target):
+        pl.semaphore_signal(semaphore, inc=1, device_id=target, device_id_type=MESH)
+
+    def load_small(i):
+        src, dst = ((qgain_in, qgain_ref), (kgain_in, kgain_ref), (freq_in, freq_ref))[i]
+        return pltpu.make_async_copy(src, dst, small_sem.at[i])
+
+    for i in range(3):
+        load_small(i).start()
+
     barrier = pltpu.get_barrier_semaphore()
     greeted = [column_device(dy, dc) for dy, dc in column_peers]
-    greeted += [after, before]
-    greeted += [z_device(dz) for dz in range(1, NZ)]
-    greeted += [x_device(dx) for dx in range(1, NX)]
+    greeted += [before, z_device(NZ - 1), x_device(NX - 1)]
     for target in greeted:
-        pl.semaphore_signal(barrier, inc=1, device_id=target, device_id_type=MESH)
+        greet(barrier, target)
     pl.semaphore_wait(barrier, len(greeted))
+    greet(relay_up, z_device(1))
+    greet(relay_up, x_device(1))
 
     def remote(src, dst, send, recv, target):
         return pltpu.make_async_remote_copy(
@@ -200,6 +218,9 @@
     core_copies[3].wait_recv()
     spread("qg", [(0, st_qg.at[0]), (0, st_qg.at[1])], 2 * D, qg, 0, qg_send, qg_recv, theirs, 1)
 
+    for i in range(3):
+        load_small(i).wait()
+
     first_token = col * (NP * T) - NH * T
     half = (NP + NH) * T // 2
     step_rows = 64
@@ -249,6 +270,10 @@
         wait_kv(NH + i)
         halo_copy(i).start()
 
+    pl.semaphore_wait(relay_up, 2)
+    for target in (z_device(1), z_device(NZ - 1), x_device(1), x_device(NX - 1)):
+        greet(relay_one, target)
+
     @pl.loop(0, NH)
     def _(i):
         wait_kv(i)
@@ -256,6 +281,10 @@
     @pl.loop(NH, NH + NP)
     def _(block):
         prepare_keys(block)
+
+    pl.semaphore_wait(relay_one, 4)
+    greet(relay_two, z_device(2))
+    greet(relay_two, z_device(NZ - 2))
 
     halo_valid = jnp.where(col == 0, 0.0, 1.0)
     key_row = lax.broadcasted_iota(jnp.int32, (T, 2 * T), 0)
@@ -273,36 +302,31 @@
     def owner(block):
         return 2 * (block // 4) + block % 2, (block // 2) % 2
 
-    def dq_copies(block):
+    def dq_parts(block):
         yy, cc = owner(block)
-        src = dq_res.at[block]
-        dst = plane_q.at[cc, :, cols_of(y * 2 * D, 2 * D)]
-        return (
-            remote(src, dst, dq_send.at[block], dq_recv.at[y, cc], device(col, yy, c)),
-            pltpu.make_async_copy(src, dst, dq_recv.at[y, cc]),
-            yy,
-        )
-
-    def dkv_copies(block):
+        return dq_res.at[block], plane_q.at[cc, :, cols_of(y * 2 * D, 2 * D)], dq_send.at[block], dq_recv.at[y, cc], yy
+
+    def dkv_parts(block):
         yy, cc = owner(block)
-        src = dkv_res.at[block]
-        dst = plane_kv.at[cc, :, :, cols_of(y * D, D)]
-        return (
-            remote(src, dst, dkv_send.at[block], dkv_recv.at[y, cc], device(col, yy, c)),
-            pltpu.make_async_copy(src, dst, dkv_recv.at[y, cc]),
-            yy,
-        )
-
-    def give(copies):
-        far, near, yy = copies
+        return dkv_res.at[block], plane_kv.at[cc, :, :, cols_of(y * D, D)], dkv_send.at[block], dkv_recv.at[y, cc], yy
+
+    def give(parts):
+        src, dst, send, recv, yy = parts
 
         @pl.when(yy == y)
         def _():
-            near.start()
+            pltpu.make_async_copy(src, dst, recv).start()
 
         @pl.when(yy != y)
         def _():
-            far.start()
+            remote(src, dst, send, recv, device(col, yy, c)).start()
+
+    def given(parts):
+        src, dst, send, recv, yy = parts
+
+        @pl.when(yy != y)
+        def _():
+            remote(src, dst, send, recv, device(col, yy, c)).wait_send()
 
     def attend(block):
         rows = rows_of(block)
@@ -347,44 +371,42 @@
             grad, term = norm_back(turned, raw[h], qgain, cosine, sine)
             dq_res[block, :, h * D : (h + 1) * D] = grad
             terms[0:1] += term
-        give(dq_copies(block))
-
-    @pl.loop(NH, NP)
-    def _(block):
-        attend(block)
+
+    def in_turn(i):
+        pair = i // 2
+        core = pair // 2 + c - 2 * (pair // 2) * c
+        return 4 * (1 - pair % 2) + 2 * core + i % 2
+
+    @pl.loop(0, 2)
+    def _(i):
+        attend(in_turn(i))
 
     @pl.loop(0, NH)
     def _(i):
         halo_copy(i).wait_recv()
         prepare_keys(i)
 
+    pl.semaphore_wait(relay_two, 2)
+    greet(relay_four, z_device(4))
+    greet(relay_four, z_device(NZ - 4))
+
+    @pl.loop(2, NP)
+    def _(i):
+        attend(in_turn(i))
+
     def return_copy(i):
         return remote(halo_res.at[i], halo_ret.at[i], ret_send.at[i], ret_recv.at[i], before)
 
     @pl.loop(0, NH)
     def _(block):
-        attend(block)
         keys = rows_of(block)
-        grad_key = dkv[0, keys] * LN2
-        halo_res[block, 0] = grad_key.astype(BF16)
+        halo_res[block, 0] = (dkv[0, keys] * LN2).astype(BF16)
         halo_res[block, 1] = dkv[1, keys].astype(BF16)
         return_copy(block).start()
-        unit, _ = unit_of(kv[0, keys].astype(F32))
-        w = rope_back(grad_key, ctab[keys], stab[keys])
-        terms[1:2] += jnp.sum(w * unit, axis=0, keepdims=True)
-
-    @pl.loop(0, NH)
+
+    @pl.loop(0, NH + NP)
     def _(block):
-        keys = rows_of(block + NH)
-        grad, term = norm_back(dkv[0, keys] * LN2, kv[0, keys].astype(F32), kgain, ctab[keys], stab[keys])
-        dkv_res[block, 0] = grad
-        dkv_res[block, 1] = dkv[1, keys].astype(BF16)
-        terms[1:2] += term
-        give(dkv_copies(block))
-
-    @pl.loop(NH, NP)
-    def _(block):
-        keys = rows_of(block + NH)
+        keys = rows_of(block)
         unit, _ = unit_of(kv[0, keys].astype(F32))
         w = rope_back(dkv[0, keys] * LN2, ctab[keys], stab[keys])
         terms[1:2] += jnp.sum(w * unit, axis=0, keepdims=True)
@@ -396,23 +418,38 @@
     ]
     for copy in stage_a:
         copy.start()
+
+    @pl.loop(0, NP)
+    def _(block):
+        give(dq_parts(block))
+
     for dy, dc in column_peers:
         slot = place((y + dy) % 4, (c + dc) % 2)
         pltpu.make_async_copy(ar_a.at[slot], ar_a.at[slot], ara_recv.at[slot]).wait()
-    ar_b[z] = jnp.sum(ar_a[...], axis=0)
+    ar_c[x] = jnp.sum(ar_a[...], axis=0)
+    stage_c = [
+        remote(ar_c.at[x], ar_c.at[x], arc_send.at[dx], arc_recv.at[x], x_device(dx)) for dx in range(1, NX)
+    ]
+    for copy in stage_c:
+        copy.start()
+
+    @pl.loop(0, NH)
+    def _(block):
+        keys = rows_of(block + NH)
+        grad, _ = norm_back(dkv[0, keys] * LN2, kv[0, keys].astype(F32), kgain, ctab[keys], stab[keys])
+        dkv_res[block, 0] = grad
+        dkv_res[block, 1] = dkv[1, keys].astype(BF16)
+        give(dkv_parts(block))
+
+    pl.semaphore_wait(relay_four, 2)
+    for dx in range(1, NX):
+        slot = (x + dx) % NX
+        pltpu.make_async_copy(ar_c.at[slot], ar_c.at[slot], arc_recv.at[slot]).wait()
+    ar_b[z] = jnp.sum(ar_c[...], axis=0)
     stage_b = [
         remote(ar_b.at[z], ar_b.at[z], arb_send.at[dz], arb_recv.at[z], z_device(dz)) for dz in range(1, NZ)
     ]
     for copy in stage_b:
-        copy.start()
-    for dz in range(1, NZ):
-        slot = (z + dz) % NZ
-        pltpu.make_async_copy(ar_b.at[slot], ar_b.at[slot], arb_recv.at[slot]).wait()
-    ar_c[x] = jnp.sum(ar_b[...], axis=0)
-    stage_c = [
-        remote(ar_c.at[x], ar_c.at[x], arc_send.at[dx], arc_recv.at[x], x_device(dx)) for dx in range(1, NX)
-    ]
-    for copy in stage_c:
         copy.start()
 
     @pl.loop(NH, NP)
@@ -423,7 +460,7 @@
         grad, _ = norm_back(grad_key, kv[0, keys].astype(F32), kgain, ctab[keys], stab[keys])
         dkv_res[block, 0] = grad
         dkv_res[block, 1] = (dkv[1, keys] + halo_ret[block - NH, 1].astype(F32)).astype(BF16)
-        give(dkv_copies(block))
+        give(dkv_parts(block))
 
     wide, narrow = cols_of(c * 8 * D, 8 * D), cols_of(c * 4 * D, 4 * D)
     plane_parts = (
@@ -449,13 +486,6 @@
         stay.start()
         out_copies.append((away, stay))
 
-    for dx in range(1, NX):
-        slot = (x + dx) % NX
-        pltpu.make_async_copy(ar_c.at[slot], ar_c.at[slot], arc_recv.at[slot]).wait()
-    gains = jnp.sum(ar_c[...], axis=0)
-    qterm_out[...] = gains[0:1]
-    kterm_out[...] = gains[1:2]
-
     for copy in core_copies + sends + stage_a + stage_b + stage_c:
         copy.wait_send()
 
@@ -466,37 +496,54 @@
 
     @pl.loop(0, NP)
     def _(block):
-        yy, _ = owner(block)
-
-        @pl.when(yy != y)
-        def _():
-            dq_copies(block)[0].wait_send()
-            dkv_copies(block)[0].wait_send()
+        given(dq_parts(block))
+        given(dkv_parts(block))
 
     for away, stay in out_copies:
         away.wait()
         stay.wait()
 
+    for dz in range(1, NZ):
+        slot = (z + dz) % NZ
+        pltpu.make_async_copy(ar_b.at[slot], ar_b.at[slot], arb_recv.at[slot]).wait()
+    gains = jnp.sum(ar_b[...], axis=0)
+    qterm_out[...] = gains[0:1]
+    kterm_out[...] = gains[1:2]
+
+
+def deliver(*refs):
+    n = (len(refs) - 1) // 2
+    copies = [pltpu.make_async_copy(refs[i], refs[n + i], refs[-1].at[i]) for i in range(n)]
+    for copy in copies:
+        copy.start()
+    for copy in copies:
+        copy.wait()
+
 
 def per_device(query_input, key_input, saved_value_input, grad_output, query_gain, key_gain):
     frequency = (10000.0 ** (-np.arange(64, dtype=np.float64) / 64)).astype(np.float32)
     frequency = jnp.asarray(np.concatenate([frequency, frequency])[None, :])
-    anywhere = pl.BlockSpec(memory_space=pl.ANY)
     vmem = pl.BlockSpec(memory_space=pltpu.VMEM)
     dma = pltpu.SemaphoreType.DMA
+    regular = pltpu.SemaphoreType.REGULAR
     span = (NP + NH) * T
-    dq, dk, dv, qterm, kterm = pl.pallas_call(
+    held = pl.BlockSpec(memory_space=pltpu.HBM)
+    shapes = (
+        jax.ShapeDtypeStruct((T, 16 * D), BF16),
+        jax.ShapeDtypeStruct((T, 8 * D), BF16),
+        jax.ShapeDtypeStruct((T, 8 * D), BF16),
+        jax.ShapeDtypeStruct((1, D), F32),
+        jax.ShapeDtypeStruct((1, D), F32),
+    )
+    results = pl.pallas_call(
         kernel,
-        out_shape=(
-            jax.ShapeDtypeStruct((T, 16 * D), BF16),
-            jax.ShapeDtypeStruct((T, 8 * D), BF16),
-            jax.ShapeDtypeStruct((T, 8 * D), BF16),
-            jax.ShapeDtypeStruct((1, D), F32),
-            jax.ShapeDtypeStruct((1, D), F32),
-        ),
-        in_specs=[anywhere] * 4 + [vmem] * 3,
-        out_specs=(anywhere, anywhere, anywhere, vmem, vmem),
+        out_shape=shapes,
+        in_specs=[held] * 7,
+        out_specs=(vmem,) * 5,
         scratch_shapes=[
+            pltpu.VMEM((1, D), F32),
+            pltpu.VMEM((1, D), F32),
+            pltpu.VMEM((1, D), F32),
             pltpu.VMEM((2, T, 4 * D), BF16),
             pltpu.VMEM((2, T, 8 * D), BF16),
             pltpu.VMEM((2, span, D), BF16),
@@ -541,9 +588,14 @@
             dma((NZ,)),
             dma((NX,)),
             dma((NX,)),
+            dma((3,)),
+            regular,
+            regular,
+            regular,
+            regular,
         ],
         compiler_params=pltpu.CompilerParams(
-            collective_id=0, has_side_effects=True, vmem_limit_bytes=40 * 2**20
+            collective_id=0, has_side_effects=True, vmem_limit_bytes=61 * 2**20
         ),
         cost_estimate=pl.CostEstimate(flops=1700000000, bytes_accessed=3000000, transcendentals=1400000),
     )(
@@ -555,6 +607,13 @@
         key_gain.reshape(1, D),
         frequency,
     )
+    dq, dk, dv, qterm, kterm = pl.pallas_call(
+        deliver,
+        out_shape=shapes,
+        in_specs=[vmem] * 5,
+        out_specs=(held,) * 5,
+        scratch_shapes=[dma((5,))],
+    )(*results)
     return dq, dk, dv, qterm.reshape(D), kterm.reshape(D)
 
 

time: 77.4 us -> 59.2 us (0.76)
  the two profiles are of different devices: /device:TPU:27 before, /device:TPU:1 now
where the time goes in v2:
time: 59.2 us; the launch traced here: 58.7 us
  Pallas kernels  58.1 us (98%)
  between operations  0.64 us (1%)
    pallas_call x1, Pallas kernels, per_device(): pl.pallas_call(kernel, out_shape=shapes, in_specs=[held] * 7, out_specs=(...  55.9 us
    pallas_call x1, Pallas kernels, per_device(): pl.pallas_call(deliver, out_shape=shapes, in_specs=[vmem] * 5, out_specs=...  2.2 us

profile of v2, /device:TPU:1, one launch (start us, length us, event | category | flops | bytes accessed | tf_op | source)
XLA Modules:
  0.0 58.7 jit_solution(5397335402628174413)
XLA Ops:
  0.6 55.9 %shard_map.110 = (bf16[128,2048]{1,0:T(8,128)(2,1)}, bf16[128,1024]{1,0:T(8,128)(2,1)}, bf16[128,1024]{1,0:T(8,128)(2,1)}, f32[1,128]{1,0:T(1,128)}, f32[1,128]{1,0:T(1,128)}) custom-call(bf16[128,2048]{1,0:T(8,128)(2,1)} %q_in.1, bf16[128,1024]{1,0:T(8,128)(2,1)} %k_in.1, bf16[128,1024]{1,0:T(8,128)(2,1)} %v_in.1, bf16[128,2048]{1,0:T(8,128)(2,1)} %g_in.1, ...), custom_call_target="tpu_custom_call" | custom-call | flops 1700000000 | bytes 3000000 | tf_op jit(solution)/shard_map/pallas_call | solution.py:538
  56.5 2.2 %shard_map.111 = (bf16[128,2048]{1,0:T(8,128)(2,1)}, bf16[128,1024]{1,0:T(8,128)(2,1)}, bf16[128,1024]{1,0:T(8,128)(2,1)}, f32[1,128]{1,0:T(1,128)}, f32[1,128]{1,0:T(1,128)}) custom-call(bf16[128,2048]{1,0:T(8,128)(2,1)} %get-tuple-element.15.refs_0_, bf16[128,1024]{1,0:T(8,128)(2,1)} %get-tuple-element.16.refs_1_, ...), custom_call_target="tpu_custom_call" | custom-call | tf_op jit(solution)/shard_map/pallas_call | solution.py:610

commit v3 on v2

--- a/solution.py
+++ b/solution.py
@@ -31,8 +31,8 @@
     return 4 * (y // 2) + 2 * c + y % 2
 
 
-def rows_of(block):
-    return pl.ds(pl.multiple_of(block * T, T), T)
+def rows_of(block, blocks=1):
+    return pl.ds(pl.multiple_of(block * T, T), blocks * T)
 
 
 def cols_of(start, size):
@@ -86,6 +86,8 @@
     stab,
     weights,
     gprobs,
+    probs_low,
+    grad_scores,
     dkv,
     dq_res,
     dkv_res,
@@ -259,14 +261,16 @@
         )
 
     def prepare_keys(block):
-        rows = rows_of(block)
+        rows = rows_of(block, NH)
         unit, _ = unit_of(kv[0, rows].astype(F32))
         turned = rope(unit * kgain, ctab[rows], stab[rows])
         kready[rows] = turned.astype(BF16)
-        ktrans[block] = turned.T.astype(BF16)
+        ktrans[:, cols_of(block * T, NH * T)] = turned.T.astype(BF16)
 
     @pl.loop(0, NH)
-    def _(i):
+    def _(turn):
+        core = turn // 2 + c - 2 * (turn // 2) * c
+        i = 2 * core + turn % 2
         wait_kv(NH + i)
         halo_copy(i).start()
 
@@ -278,9 +282,8 @@
     def _(i):
         wait_kv(i)
 
-    @pl.loop(NH, NH + NP)
-    def _(block):
-        prepare_keys(block)
+    prepare_keys(NH)
+    prepare_keys(2 * NH)
 
     pl.semaphore_wait(relay_one, 4)
     greet(relay_two, z_device(2))
@@ -340,59 +343,61 @@
             [(rope(unit_of(r)[0] * qgain, cosine, sine) * (SCALE * LOG2E)).astype(BF16) for r in raw], axis=0
         )
         grads = jnp.concatenate([qg[1, rows, h * D : (h + 1) * D] for h in range(2)], axis=0)
+        window = pl.ds(pl.multiple_of(block * T, T), (NH + 1) * T)
+        weights[...] = dot_nt(kready[window], queries)
+        gprobs[...] = dot_nt(kv[1, window], grads)
         total = jnp.zeros((1, 2 * T), F32)
         inner = jnp.zeros((1, 2 * T), F32)
         for t in range(NH + 1):
-            keys = rows_of(block + t)
-            weight = jnp.exp2(dot_nt(kready[keys], queries))
+            part = slice(t * T, (t + 1) * T)
+            weight = jnp.exp2(weights[part])
             if t == 0:
                 weight = jnp.where(newer, weight, 0.0)
             if t == NH:
                 weight = jnp.where(newer, 0.0, weight)
             else:
                 weight = weight * jnp.where(block + t < NH, halo_valid, 1.0)
-            grad_prob = dot_nt(kv[1, keys], grads)
             total = total + jnp.sum(weight, axis=0, keepdims=True)
-            inner = inner + jnp.sum(weight * grad_prob, axis=0, keepdims=True)
-            weights[t] = weight
-            gprobs[t] = grad_prob
+            inner = inner + jnp.sum(weight * gprobs[part], axis=0, keepdims=True)
+            weights[part] = weight
         inverse = 1.0 / total
         inner = inner * inverse
-        grad_query = jnp.zeros((D, 2 * T), F32)
         for t in range(NH + 1):
-            keys = rows_of(block + t)
-            prob = weights[t] * inverse
-            grad_score = (prob * (gprobs[t] - inner)).astype(BF16)
-            dkv[1, keys] += dot_nn(prob.astype(BF16), grads)
-            dkv[0, keys] += dot_nn(grad_score, queries)
-            grad_query = grad_query + dot_nn(ktrans[block + t], grad_score)
+            part = slice(t * T, (t + 1) * T)
+            prob = weights[part] * inverse
+            probs_low[part] = prob.astype(BF16)
+            grad_scores[part] = (prob * (gprobs[part] - inner)).astype(BF16)
+        dkv[1, window] += dot_nn(probs_low[...], grads)
+        dkv[0, window] += dot_nn(grad_scores[...], queries)
+        grad_query = dot_nn(ktrans[:, cols_of(block * T, (NH + 1) * T)], grad_scores[...])
         for h in range(2):
             turned = grad_query[:, h * T : (h + 1) * T].T * SCALE
             grad, term = norm_back(turned, raw[h], qgain, cosine, sine)
             dq_res[block, :, h * D : (h + 1) * D] = grad
             terms[0:1] += term
 
-    def in_turn(i):
-        pair = i // 2
-        core = pair // 2 + c - 2 * (pair // 2) * c
-        return 4 * (1 - pair % 2) + 2 * core + i % 2
-
-    @pl.loop(0, 2)
+    late = jnp.where(z == 0, 1, 0)
+    halo_turn = 2 + 2 * late
+
+    @pl.loop(0, NP)
     def _(i):
-        attend(in_turn(i))
-
-    @pl.loop(0, NH)
-    def _(i):
-        halo_copy(i).wait_recv()
-        prepare_keys(i)
-
-    pl.semaphore_wait(relay_two, 2)
-    greet(relay_four, z_device(4))
-    greet(relay_four, z_device(NZ - 4))
-
-    @pl.loop(2, NP)
-    def _(i):
-        attend(in_turn(i))
+        @pl.when(i == halo_turn)
+        def _():
+            @pl.loop(0, NH)
+            def _(j):
+                halo_copy(j).wait_recv()
+
+            prepare_keys(0)
+
+            pl.semaphore_wait(relay_two, 2)
+            greet(relay_four, z_device(4))
+            greet(relay_four, z_device(NZ - 4))
+
+        major, minor = i // 4, (i // 2) % 2
+        first = late * major + (1 - late) * minor
+        swapped = late * minor + (1 - late) * major
+        core = swapped + c - 2 * swapped * c
+        attend(4 * (1 - first) + 2 * core + i % 2)
 
     def return_copy(i):
         return remote(halo_res.at[i], halo_ret.at[i], ret_send.at[i], ret_recv.at[i], before)
@@ -404,9 +409,9 @@
         halo_res[block, 1] = dkv[1, keys].astype(BF16)
         return_copy(block).start()
 
-    @pl.loop(0, NH + NP)
-    def _(block):
-        keys = rows_of(block)
+    @pl.loop(0, (NH + NP) // NH)
+    def _(part):
+        keys = rows_of(part * NH, NH)
         unit, _ = unit_of(kv[0, keys].astype(F32))
         w = rope_back(dkv[0, keys] * LN2, ctab[keys], stab[keys])
         terms[1:2] += jnp.sum(w * unit, axis=0, keepdims=True)
@@ -422,7 +427,6 @@
     @pl.loop(0, NP)
     def _(block):
         give(dq_parts(block))
-
     for dy, dc in column_peers:
         slot = place((y + dy) % 4, (c + dc) % 2)
         pltpu.make_async_copy(ar_a.at[slot], ar_a.at[slot], ara_recv.at[slot]).wait()
@@ -433,12 +437,14 @@
     for copy in stage_c:
         copy.start()
 
+
+    keys = rows_of(NH, NH)
+    grad, _ = norm_back(dkv[0, keys] * LN2, kv[0, keys].astype(F32), kgain, ctab[keys], stab[keys])
+    dkv_res[0:NH, 0] = grad.reshape(NH, T, D)
+    dkv_res[0:NH, 1] = dkv[1, keys].astype(BF16).reshape(NH, T, D)
+
     @pl.loop(0, NH)
     def _(block):
-        keys = rows_of(block + NH)
-        grad, _ = norm_back(dkv[0, keys] * LN2, kv[0, keys].astype(F32), kgain, ctab[keys], stab[keys])
-        dkv_res[block, 0] = grad
-        dkv_res[block, 1] = dkv[1, keys].astype(BF16)
         give(dkv_parts(block))
 
     pl.semaphore_wait(relay_four, 2)
@@ -446,8 +452,9 @@
         slot = (x + dx) % NX
         pltpu.make_async_copy(ar_c.at[slot], ar_c.at[slot], arc_recv.at[slot]).wait()
     ar_b[z] = jnp.sum(ar_c[...], axis=0)
+    farthest_first = sorted(range(1, NZ), key=lambda dz: abs(dz - NZ // 2))
     stage_b = [
-        remote(ar_b.at[z], ar_b.at[z], arb_send.at[dz], arb_recv.at[z], z_device(dz)) for dz in range(1, NZ)
+        remote(ar_b.at[z], ar_b.at[z], arb_send.at[dz], arb_recv.at[z], z_device(dz)) for dz in farthest_first
     ]
     for copy in stage_b:
         copy.start()
@@ -537,7 +544,7 @@
     )
     results = pl.pallas_call(
         kernel,
-        out_shape=shapes,
+        out_shape=tuple(pltpu.VMEM(sh.shape, sh.dtype) for sh in shapes),
         in_specs=[held] * 7,
         out_specs=(vmem,) * 5,
         scratch_shapes=[
@@ -549,11 +556,13 @@
             pltpu.VMEM((2, span, D), BF16),
             pltpu.VMEM((2, NP * T, 2 * D), BF16),
             pltpu.VMEM((span, D), BF16),
-            pltpu.VMEM((NP + NH, D, T), BF16),
+            pltpu.VMEM((D, span), BF16),
             pltpu.VMEM((span, D), F32),
             pltpu.VMEM((span, D), F32),
-            pltpu.VMEM((NH + 1, T, 2 * T), F32),
-            pltpu.VMEM((NH + 1, T, 2 * T), F32),
+            pltpu.VMEM(((NH + 1) * T, 2 * T), F32),
+            pltpu.VMEM(((NH + 1) * T, 2 * T), F32),
+            pltpu.VMEM(((NH + 1) * T, 2 * T), BF16),
+            pltpu.VMEM(((NH + 1) * T, 2 * T), BF16),
             pltpu.VMEM((2, span, D), F32),
             pltpu.VMEM((NP, T, 2 * D), BF16),
             pltpu.VMEM((NP, 2, T, D), BF16),
@@ -610,9 +619,10 @@
     dq, dk, dv, qterm, kterm = pl.pallas_call(
         deliver,
         out_shape=shapes,
-        in_specs=[vmem] * 5,
+        in_specs=[pl.BlockSpec(memory_space=pl.ANY)] * 5,
         out_specs=(held,) * 5,
         scratch_shapes=[dma((5,))],
+        compiler_params=pltpu.CompilerParams(vmem_limit_bytes=2**20),
     )(*results)
     return dq, dk, dv, qterm.reshape(D), kterm.reshape(D)
 

time: 59.2 us -> 55.2 us (0.932)
  Pallas kernels: 58.1 us -> 54.4 us
    pallas_call x2, Pallas kernels: 58.1 us -> 54.4 us  [the longest x1 53.4 us: per_device(): pl.pallas_call(kernel, out_shape=tuple((pltpu.VMEM(sh.shape, sh.dtype) fo...]
where the time goes in v3:
time: 55.2 us; the launch traced here: 55.1 us
  Pallas kernels  54.4 us (99%)
  between operations  0.64 us (1%)
    pallas_call x1, Pallas kernels, per_device(): pl.pallas_call(kernel, out_shape=tuple((pltpu.VMEM(sh.shape, sh.dtype) fo...  53.4 us

profile of v3, /device:TPU:1, one launch (start us, length us, event | category | flops | bytes accessed | tf_op | source)
XLA Modules:
  0.0 55.1 jit_solution(17235265421000604912)
XLA Ops:
  0.6 53.4 %shard_map.110 = (bf16[128,2048]{1,0:T(8,128)(2,1)S(1)}, bf16[128,1024]{1,0:T(8,128)(2,1)S(1)}, bf16[128,1024]{1,0:T(8,128)(2,1)S(1)}, f32[1,128]{1,0:T(1,128)S(1)}, f32[1,128]{1,0:T(1,128)S(1)}) custom-call(bf16[128,2048]{1,0:T(8,128)(2,1)} %q_in.1, bf16[128,1024]{1,0:T(8,128)(2,1)} %k_in.1, bf16[128,1024]{1,0:T(8,128)(2,1)} %v_in.1, ...), custom_call_target="tpu_custom_call" | custom-call | flops 1700000000 | bytes 3000000 | tf_op jit(solution)/shard_map/pallas_call | solution.py:545
  54.0 1.0 %shard_map.111 = (bf16[128,2048]{1,0:T(8,128)(2,1)}, bf16[128,1024]{1,0:T(8,128)(2,1)}, bf16[128,1024]{1,0:T(8,128)(2,1)}, f32[1,128]{1,0:T(1,128)}, f32[1,128]{1,0:T(1,128)}) custom-call(bf16[128,2048]{1,0:T(8,128)(2,1)S(1)} %get-tuple-element.15.refs_0_, bf16[128,1024]{1,0:T(8,128)(2,1)S(1)} %get-tuple-element.16.refs_1_, ...), custom_call_target="tpu_custom_call" | custom-call | tf_op jit(solution)/shard_map/pallas_call | solution.py:619

commit v4 on v3

--- a/solution.py
+++ b/solution.py
@@ -81,6 +81,7 @@
     kv,
     qg,
     kready,
+    kunit,
     ktrans,
     ctab,
     stab,
@@ -264,6 +265,7 @@
         rows = rows_of(block, NH)
         unit, _ = unit_of(kv[0, rows].astype(F32))
         turned = rope(unit * kgain, ctab[rows], stab[rows])
+        kunit[rows] = unit
         kready[rows] = turned.astype(BF16)
         ktrans[:, cols_of(block * T, NH * T)] = turned.T.astype(BF16)
 
@@ -331,55 +333,71 @@
         def _():
             remote(src, dst, send, recv, device(col, yy, c)).wait_send()
 
-    def attend(block):
-        rows = rows_of(block)
-        for i in range(2):
-            slot = qg.at[i, rows]
-            pltpu.make_async_copy(slot, slot, qg_recv.at[i, block]).wait()
-        own = rows_of(block + NH)
-        cosine, sine = ctab[own], stab[own]
-        raw = [qg[0, rows, h * D : (h + 1) * D].astype(F32) for h in range(2)]
-        queries = jnp.concatenate(
-            [(rope(unit_of(r)[0] * qgain, cosine, sine) * (SCALE * LOG2E)).astype(BF16) for r in raw], axis=0
-        )
-        grads = jnp.concatenate([qg[1, rows, h * D : (h + 1) * D] for h in range(2)], axis=0)
-        window = pl.ds(pl.multiple_of(block * T, T), (NH + 1) * T)
-        weights[...] = dot_nt(kready[window], queries)
-        gprobs[...] = dot_nt(kv[1, window], grads)
-        total = jnp.zeros((1, 2 * T), F32)
-        inner = jnp.zeros((1, 2 * T), F32)
-        for t in range(NH + 1):
-            part = slice(t * T, (t + 1) * T)
-            weight = jnp.exp2(weights[part])
-            if t == 0:
-                weight = jnp.where(newer, weight, 0.0)
-            if t == NH:
-                weight = jnp.where(newer, 0.0, weight)
-            else:
-                weight = weight * jnp.where(block + t < NH, halo_valid, 1.0)
-            total = total + jnp.sum(weight, axis=0, keepdims=True)
-            inner = inner + jnp.sum(weight * gprobs[part], axis=0, keepdims=True)
-            weights[part] = weight
-        inverse = 1.0 / total
-        inner = inner * inverse
-        for t in range(NH + 1):
-            part = slice(t * T, (t + 1) * T)
-            prob = weights[part] * inverse
-            probs_low[part] = prob.astype(BF16)
-            grad_scores[part] = (prob * (gprobs[part] - inner)).astype(BF16)
-        dkv[1, window] += dot_nn(probs_low[...], grads)
-        dkv[0, window] += dot_nn(grad_scores[...], queries)
-        grad_query = dot_nn(ktrans[:, cols_of(block * T, (NH + 1) * T)], grad_scores[...])
-        for h in range(2):
-            turned = grad_query[:, h * T : (h + 1) * T].T * SCALE
-            grad, term = norm_back(turned, raw[h], qgain, cosine, sine)
-            dq_res[block, :, h * D : (h + 1) * D] = grad
-            terms[0:1] += term
+    def attend(first_block):
+        blocks = [first_block, first_block + 1]
+        for block in blocks:
+            for i in range(2):
+                slot = qg.at[i, rows_of(block)]
+                pltpu.make_async_copy(slot, slot, qg_recv.at[i, block]).wait()
+        raws, queries, grads, turns = [], [], [], []
+        for block in blocks:
+            rows, own = rows_of(block), rows_of(block + NH)
+            cosine, sine = ctab[own], stab[own]
+            raw = [qg[0, rows, h * D : (h + 1) * D].astype(F32) for h in range(2)]
+            turned = [(rope(unit_of(r)[0] * qgain, cosine, sine) * (SCALE * LOG2E)).astype(BF16) for r in raw]
+            raws.append(raw)
+            turns.append((cosine, sine))
+            queries.append(jnp.concatenate(turned, axis=0))
+            grads.append(jnp.concatenate([qg[1, rows, h * D : (h + 1) * D] for h in range(2)], axis=0))
+        for n, block in enumerate(blocks):
+            window = rows_of(block, NH + 1)
+            weights[n] = dot_nt(kready[window], queries[n])
+            gprobs[n] = dot_nt(kv[1, window], grads[n])
+        sums = []
+        for n, block in enumerate(blocks):
+            total = jnp.zeros((1, 2 * T), F32)
+            inner = jnp.zeros((1, 2 * T), F32)
+            for t in range(NH + 1):
+                part = slice(t * T, (t + 1) * T)
+                weight = jnp.exp2(weights[n, part])
+                if t == 0:
+                    weight = jnp.where(newer, weight, 0.0)
+                if t == NH:
+                    weight = jnp.where(newer, 0.0, weight)
+                else:
+                    weight = weight * jnp.where(block + t < NH, halo_valid, 1.0)
+                total = total + jnp.sum(weight, axis=0, keepdims=True)
+                inner = inner + jnp.sum(weight * gprobs[n, part], axis=0, keepdims=True)
+                weights[n, part] = weight
+            inverse = 1.0 / total
+            sums.append((inverse, inner * inverse))
+        for n, block in enumerate(blocks):
+            inverse, inner = sums[n]
+            for t in range(NH + 1):
+                part = slice(t * T, (t + 1) * T)
+                prob = weights[n, part] * inverse
+                probs_low[n, part] = prob.astype(BF16)
+                grad_scores[n, part] = (prob * (gprobs[n, part] - inner)).astype(BF16)
+        grad_query = [
+            dot_nn(ktrans[:, cols_of(block * T, (NH + 1) * T)], grad_scores[n]) for n, block in enumerate(blocks)
+        ]
+        for n, block in enumerate(blocks):
+            window = rows_of(block, NH + 1)
+            dkv[1, window] += dot_nn(probs_low[n], grads[n])
+            dkv[0, window] += dot_nn(grad_scores[n], queries[n])
+        terms_here = jnp.zeros((1, D), F32)
+        for n, block in enumerate(blocks):
+            for h in range(2):
+                turned = grad_query[n][:, h * T : (h + 1) * T].T * SCALE
+                grad, term = norm_back(turned, raws[n][h], qgain, *turns[n])
+                dq_res[block, :, h * D : (h + 1) * D] = grad
+                terms_here = terms_here + term
+        terms[0:1] += terms_here
 
     late = jnp.where(z == 0, 1, 0)
-    halo_turn = 2 + 2 * late
-
-    @pl.loop(0, NP)
+    halo_turn = 1 + late
+
+    @pl.loop(0, NP // 2)
     def _(i):
         @pl.when(i == halo_turn)
         def _():
@@ -393,11 +411,11 @@
             greet(relay_four, z_device(4))
             greet(relay_four, z_device(NZ - 4))
 
-        major, minor = i // 4, (i // 2) % 2
+        major, minor = i // 2, i % 2
         first = late * major + (1 - late) * minor
         swapped = late * minor + (1 - late) * major
         core = swapped + c - 2 * swapped * c
-        attend(4 * (1 - first) + 2 * core + i % 2)
+        attend(4 * (1 - first) + 2 * core)
 
     def return_copy(i):
         return remote(halo_res.at[i], halo_ret.at[i], ret_send.at[i], ret_recv.at[i], before)
@@ -412,9 +430,8 @@
     @pl.loop(0, (NH + NP) // NH)
     def _(part):
         keys = rows_of(part * NH, NH)
-        unit, _ = unit_of(kv[0, keys].astype(F32))
         w = rope_back(dkv[0, keys] * LN2, ctab[keys], stab[keys])
-        terms[1:2] += jnp.sum(w * unit, axis=0, keepdims=True)
+        terms[1:2] += jnp.sum(w * kunit[keys], axis=0, keepdims=True)
 
     ar_a[mine] = terms[...]
     stage_a = [
@@ -556,13 +573,14 @@
             pltpu.VMEM((2, span, D), BF16),
             pltpu.VMEM((2, NP * T, 2 * D), BF16),
             pltpu.VMEM((span, D), BF16),
+            pltpu.VMEM((span, D), F32),
             pltpu.VMEM((D, span), BF16),
             pltpu.VMEM((span, D), F32),
             pltpu.VMEM((span, D), F32),
-            pltpu.VMEM(((NH + 1) * T, 2 * T), F32),
-            pltpu.VMEM(((NH + 1) * T, 2 * T), F32),
-            pltpu.VMEM(((NH + 1) * T, 2 * T), BF16),
-            pltpu.VMEM(((NH + 1) * T, 2 * T), BF16),
+            pltpu.VMEM((2, (NH + 1) * T, 2 * T), F32),
+            pltpu.VMEM((2, (NH + 1) * T, 2 * T), F32),
+            pltpu.VMEM((2, (NH + 1) * T, 2 * T), BF16),
+            pltpu.VMEM((2, (NH + 1) * T, 2 * T), BF16),
             pltpu.VMEM((2, span, D), F32),
             pltpu.VMEM((NP, T, 2 * D), BF16),
             pltpu.VMEM((NP, 2, T, D), BF16),

time: 55.2 us -> 54.6 us (0.989)
  Pallas kernels: 54.4 us -> 53.8 us
    pallas_call x1, Pallas kernels: 53.4 us -> 52.8 us  [per_device(): pl.pallas_call(kernel, out_shape=tuple((pltpu.VMEM(sh.shape, sh.dtype) fo...]
where the time goes in v4:
time: 54.6 us; the launch traced here: 54.4 us
  Pallas kernels  53.8 us (99%)
  between operations  0.64 us (1%)
    pallas_call x1, Pallas kernels, per_device(): pl.pallas_call(kernel, out_shape=tuple((pltpu.VMEM(sh.shape, sh.dtype) fo...  52.8 us

profile of v4, /device:TPU:1, one launch (start us, length us, event | category | flops | bytes accessed | tf_op | source)
XLA Modules:
  0.0 54.4 jit_solution(7015384522946982031)
XLA Ops:
  0.6 52.8 %shard_map.110 = (bf16[128,2048]{1,0:T(8,128)(2,1)S(1)}, bf16[128,1024]{1,0:T(8,128)(2,1)S(1)}, bf16[128,1024]{1,0:T(8,128)(2,1)S(1)}, f32[1,128]{1,0:T(1,128)S(1)}, f32[1,128]{1,0:T(1,128)S(1)}) custom-call(bf16[128,2048]{1,0:T(8,128)(2,1)} %q_in.1, bf16[128,1024]{1,0:T(8,128)(2,1)} %k_in.1, bf16[128,1024]{1,0:T(8,128)(2,1)} %v_in.1, ...), custom_call_target="tpu_custom_call" | custom-call | flops 1700000000 | bytes 3000000 | tf_op jit(solution)/shard_map/pallas_call | solution.py:562
  53.4 1.0 %shard_map.111 = (bf16[128,2048]{1,0:T(8,128)(2,1)}, bf16[128,1024]{1,0:T(8,128)(2,1)}, bf16[128,1024]{1,0:T(8,128)(2,1)}, f32[1,128]{1,0:T(1,128)}, f32[1,128]{1,0:T(1,128)}) custom-call(bf16[128,2048]{1,0:T(8,128)(2,1)S(1)} %get-tuple-element.15.refs_0_, bf16[128,1024]{1,0:T(8,128)(2,1)S(1)} %get-tuple-element.16.refs_1_, ...), custom_call_target="tpu_custom_call" | custom-call | tf_op jit(solution)/shard_map/pallas_call | solution.py:637

commit v5 on v4

--- a/solution.py
+++ b/solution.py
@@ -415,7 +415,10 @@
         first = late * major + (1 - late) * minor
         swapped = late * minor + (1 - late) * major
         core = swapped + c - 2 * swapped * c
-        attend(4 * (1 - first) + 2 * core)
+        block = 4 * (1 - first) + 2 * core
+        attend(block)
+        give(dq_parts(block))
+        give(dq_parts(block + 1))
 
     def return_copy(i):
         return remote(halo_res.at[i], halo_ret.at[i], ret_send.at[i], ret_recv.at[i], before)
@@ -441,9 +444,6 @@
     for copy in stage_a:
         copy.start()
 
-    @pl.loop(0, NP)
-    def _(block):
-        give(dq_parts(block))
     for dy, dc in column_peers:
         slot = place((y + dy) % 4, (c + dc) % 2)
         pltpu.make_async_copy(ar_a.at[slot], ar_a.at[slot], ara_recv.at[slot]).wait()

time: 54.6 us -> 54.4 us (level)
  no operation moved by 1% of the time
where the time goes in v5:
time: 54.4 us; the launch traced here: 54.3 us
  Pallas kernels  53.7 us (99%)
  between operations  0.64 us (1%)
    pallas_call x1, Pallas kernels, per_device(): pl.pallas_call(kernel, out_shape=tuple((pltpu.VMEM(sh.shape, sh.dtype) fo...  52.7 us

profile of v5, /device:TPU:1, one launch (start us, length us, event | category | flops | bytes accessed | tf_op | source)
XLA Modules:
  0.0 54.3 jit_solution(1377095024655050548)
XLA Ops:
  0.6 52.7 %shard_map.110 = (bf16[128,2048]{1,0:T(8,128)(2,1)S(1)}, bf16[128,1024]{1,0:T(8,128)(2,1)S(1)}, bf16[128,1024]{1,0:T(8,128)(2,1)S(1)}, f32[1,128]{1,0:T(1,128)S(1)}, f32[1,128]{1,0:T(1,128)S(1)}) custom-call(bf16[128,2048]{1,0:T(8,128)(2,1)} %q_in.1, bf16[128,1024]{1,0:T(8,128)(2,1)} %k_in.1, bf16[128,1024]{1,0:T(8,128)(2,1)} %v_in.1, ...), custom_call_target="tpu_custom_call" | custom-call | flops 1700000000 | bytes 3000000 | tf_op jit(solution)/shard_map/pallas_call | solution.py:562
  53.3 1.0 %shard_map.111 = (bf16[128,2048]{1,0:T(8,128)(2,1)}, bf16[128,1024]{1,0:T(8,128)(2,1)}, bf16[128,1024]{1,0:T(8,128)(2,1)}, f32[1,128]{1,0:T(1,128)}, f32[1,128]{1,0:T(1,128)}) custom-call(bf16[128,2048]{1,0:T(8,128)(2,1)S(1)} %get-tuple-element.15.refs_0_, bf16[128,1024]{1,0:T(8,128)(2,1)S(1)} %get-tuple-element.16.refs_1_, ...), custom_call_target="tpu_custom_call" | custom-call | tf_op jit(solution)/shard_map/pallas_call | solution.py:637
